TPU v7x, 512 devices: a whole 4x8x8 slice. The times are simulated.
512 devices in a mesh: rep: 32 (over z_hi, y, core), shard: 16 (over z_lo, x).
Axes of the slice: x: 4, y: 8, z: 8 (z_hi: 2, z_lo: 4; z = z_hi * 4 + z_lo), core: 2. Of those that a mesh axis runs over, the one named last changes fastest.
Arguments:
- queries: bfloat16 [65536, 4096], P(('rep', 'shard')), may hold values from -120 to 120
- keys: bfloat16 [65536, 512], P(('rep', 'shard')), may hold values from -5.5 to 5.5
- grad_out: bfloat16 [65536, 4096], P(('rep', 'shard')), may hold values from -0.75 to 0.75
- inputs: bfloat16 [65536, 8192], P(('rep', 'shard')), may hold values from -6 to 6
- old_owner: int32 [64], replicated, may hold values from 0 to 11, as said below
- new_owner: int32 [64], replicated, may hold values from 0 to 15, as said below
- param_old: float32 [128, 96, 512], P('rep', 'shard'), may hold values from -0.75 to 0.75
- first_old: float32 [128, 96, 512], P('rep', 'shard'), may hold values from -6 to 6
- second_old: float32 [128, 96, 512], P('rep', 'shard'), may hold values from 0.5 to 20
Outputs:
- param_new: float32 [128, 64, 512], P('rep', 'shard')
- first_new: float32 [128, 64, 512], P('rep', 'shard')
- second_new: float32 [128, 64, 512], P('rep', 'shard')
- weights: bfloat16 [128, 64, 512], P('rep')
Inputs may be any that keep to these rules, and one draw needn't show every extreme that they name: `old_owner`: each old owner holds at most 6 blocks, and some hold exactly 6. `new_owner`: each new owner holds exactly 4 blocks.
All inputs are finite; a program needn't handle non-finite values.
Results may differ from a plain program's by a relative error of at most 0.0034.
Values may be sent and summed in bfloat16 or wider, within the bound.
No kernel may reach another device: no remote copies, remote signals or barrier semaphores. Data moves between devices by JAX's collectives and lax.ppermute only.
A program may use at most 128 MiB of HBM per device.

v0:
```python
import jax
import jax.numpy as jnp
from jax import lax
from jax.sharding import PartitionSpec as P

KV = 4
HD = 128
GRP = 8
STEP = 1000
beta_first = 0.9
beta_second = 0.95
learning_rate = 0.02
decay_rate = 0.1
epsilon = 1e-08


def laid_out(parts, dim):
    shape = list(parts.shape[1:])
    shape[dim] *= parts.shape[0]
    return jnp.moveaxis(parts, 0, dim).reshape(shape)


def from_everyone(x, axis):
    copies = jnp.broadcast_to(x, (lax.axis_size(axis), *x.shape))
    return lax.all_to_all(copies, axis, split_axis=0, concat_axis=0, tiled=True)


def collect(x, axis, dim):
    return laid_out(from_everyone(x, axis), dim)


def split_up(x, dim, devices):
    shape = x.shape
    parts = x.reshape(*shape[:dim], devices, shape[dim] // devices, *shape[dim + 1 :])
    return jnp.moveaxis(parts, dim, 0)


def sent_and_summed(x, axis, dim):
    parts = split_up(x, dim, lax.axis_size(axis))
    arrived = lax.all_to_all(parts, axis, split_axis=0, concat_axis=0, tiled=True)
    return arrived.sum(axis=0)


def owner_ranks(owner, owners):
    onehot = (owner[:, None] == jnp.arange(owners, dtype=jnp.int32)[None, :]).astype(jnp.int32)
    running = jnp.cumsum(onehot, axis=0)
    return jnp.sum(running * onehot, axis=1) - 1


def slot_table(owner, owners, capacity):
    blocks = owner.shape[0]
    position = owner * capacity + owner_ranks(owner, owners)
    match = position[None, :] == jnp.arange(owners * capacity, dtype=jnp.int32)[:, None]
    chosen = jnp.sum(jnp.where(match, jnp.arange(blocks, dtype=jnp.int32)[None, :], 0), axis=1)
    return (chosen, jnp.any(match, axis=1))


def adamw(param, first, second, gradient):
    first = beta_first * first + (1.0 - beta_first) * gradient
    second = beta_second * second + (1.0 - beta_second) * gradient * gradient
    first_hat = first / (1.0 - beta_first**STEP)
    second_hat = second / (1.0 - beta_second**STEP)
    param = param - learning_rate * (
        first_hat / (jnp.sqrt(second_hat) + epsilon) + decay_rate * param
    )
    return (param, first, second)


def value_terms(queries, keys_all, grad_out, offset):
    rows_here = queries.shape[0]
    length = keys_all.shape[0]
    query_groups = queries.reshape(rows_here, KV, GRP, HD).transpose(1, 2, 0, 3)
    cotangent_groups = grad_out.reshape(rows_here, KV, GRP, HD).transpose(1, 2, 0, 3)
    key_groups = keys_all.reshape(length, KV, HD).transpose(1, 0, 2)
    allowed = jnp.arange(length)[None, :] <= (offset + jnp.arange(rows_here))[:, None]

    def one_group(triple):
        query_block, key_block, cotangent = triple
        scores = jnp.einsum(
            "htd,ud->htu", query_block, key_block, preferred_element_type=jnp.float32
        ) * HD ** (-0.5)
        scores = jnp.where(allowed[None], scores, -jnp.inf)
        highest = jnp.max(scores, axis=-1, keepdims=True)
        weights = jnp.exp(scores - highest)
        probs = (weights / jnp.sum(weights, axis=-1, keepdims=True)).astype(jnp.bfloat16)
        return jnp.einsum("htu,htd->ud", probs, cotangent, preferred_element_type=jnp.float32)

    return lax.map(one_group, (query_groups, key_groups, cotangent_groups))


def local(queries, keys, grad_out, inputs, old_owner, new_owner, param_old, first_old, second_old):
    shards = lax.axis_size("shard")
    replicas = lax.axis_size("rep")
    shard_index = lax.axis_index("shard")
    rows_here = queries.shape[0]
    blocks = old_owner.shape[0]
    block_rows = inputs.shape[1] // blocks
    new_capacity = blocks // shards
    columns = KV * HD
    keys_all = collect(keys, "shard", 0)
    value_part = value_terms(queries, keys_all, grad_out, shard_index * rows_here)
    values = lax.psum(value_part, "shard").astype(jnp.bfloat16)
    slot_block, slot_valid = slot_table(new_owner, shards, new_capacity)
    pieces = inputs.reshape(rows_here, blocks, block_rows)
    outgoing = jnp.where(
        slot_valid[None, :, None], jnp.take(pieces, slot_block, axis=1), jnp.zeros((), jnp.bfloat16)
    )
    arrived = lax.all_to_all(outgoing, "shard", split_axis=1, concat_axis=0, tiled=True)
    product = jnp.einsum("tsk,gtd->ksgd", arrived, values, preferred_element_type=jnp.float32)
    gradient = sent_and_summed(
        product.reshape(block_rows // replicas * lax.axis_size("rep"), new_capacity, columns),
        "rep",
        0,
    )
    new_block, unused_valid = slot_table(new_owner, shards, new_capacity)
    old_rank = owner_ranks(old_owner, shards)
    source_slot = jnp.take(old_rank, new_block)
    keeping = jnp.take(old_owner, new_block) == shard_index
    sent_param = jnp.where(keeping[None, :, None], jnp.take(param_old, source_slot, axis=1), 0.0)
    sent_first = jnp.where(keeping[None, :, None], jnp.take(first_old, source_slot, axis=1), 0.0)
    sent_second = jnp.where(keeping[None, :, None], jnp.take(second_old, source_slot, axis=1), 0.0)
    received = (
        lax.all_to_all(sent_param, "shard", split_axis=1, concat_axis=0, tiled=True),
        lax.all_to_all(sent_first, "shard", split_axis=1, concat_axis=0, tiled=True),
        lax.all_to_all(sent_second, "shard", split_axis=1, concat_axis=0, tiled=True),
    )
    moved = tuple(
        (jnp.sum(state.reshape(shards, -1, new_capacity, columns), axis=0) for state in received)
    )
    param_new, first_new, second_new = adamw(moved[0], moved[1], moved[2], gradient)
    working = param_new.astype(jnp.bfloat16)
    every_shard = collect(working, "shard", 1)
    new_slot = new_owner * new_capacity + owner_ranks(new_owner, shards)
    weights = jnp.take(every_shard, new_slot, axis=1)
    return (param_new, first_new, second_new, weights)


def solution(mesh):
    placed = (
        P(("rep", "shard"), None),
        P(("rep", "shard"), None),
        P(("rep", "shard"), None),
        P(("rep", "shard"), None),
        P(),
        P(),
        P("rep", "shard", None),
        P("rep", "shard", None),
        P("rep", "shard", None),
    )
    return jax.shard_map(
        local,
        mesh=mesh,
        in_specs=placed,
        out_specs=(
            P("rep", "shard", None),
            P("rep", "shard", None),
            P("rep", "shard", None),
            P("rep", None, None),
        ),
        check_vma=False,
    )
```

profile of v0, /device:TPU:8, one launch (start us, length us, event | category | flops | bytes accessed | tf_op | source)
XLA Modules:
  0.0 359.6 jit_solution(8832650210763158937)
XLA Ops:
  11.4 9.8 %all-to-all-start = ((f32[4,64,512]{2,0,1:T(4,128)}), f32[4,64,512]{2,0,1:T(4,128)S(1)}, u32[]{:S(2)}, u32[]{:S(2)}) async-start(f32[4,64,512]{2,0,1:T(4,128)} %get-tuple-element.130), calls=%async_computation | async-start | bytes 1048576 | tf_op jit(solution)/shard_map/all_to_all | solution.py:123
  21.4 15.3 %all-to-all-done = f32[4,64,512]{2,0,1:T(4,128)S(1)} async-done(((f32[4,64,512]{2,0,1:T(4,128)}), f32[4,64,512]{2,0,1:T(4,128)S(1)}, u32[]{:S(2)}, u32[]{:S(2)}) %all-to-all-start) | async-done | bytes 524320 | tf_op jit(solution)/shard_map/all_to_all | solution.py:123
  37.1 52.8 %all_to_all.69 = bf16[16,128,512]{1,2,0:T(8,128)(2,1)} all-to-all(bf16[16,128,512]{1,2,0:T(8,128)(2,1)S(1)} %broadcast_in_dim.138), channel_id=1, replica_groups=mesh['rep'=32,'shard'=16] {'shard'}, dimensions={0} | all-to-all | bytes 4194304 | tf_op jit(solution)/shard_map/all_to_all | solution.py:25
  89.8 4.4 %all-to-all-start.1 = ((f32[4,64,512]{2,0,1:T(4,128)}), f32[4,64,512]{2,0,1:T(4,128)S(1)}, u32[]{:S(2)}, u32[]{:S(2)}) async-start(f32[4,64,512]{2,0,1:T(4,128)} %get-tuple-element.128), calls=%async_computation.1 | async-start | bytes 1048576 | tf_op jit(solution)/shard_map/all_to_all | solution.py:124
  94.3 3.2 copy.87
  97.5 2.9 copy.88
  100.5 2.4 copy.79
  104.2 2.5 gather_fusion
  112.8 7.5 %all-to-all-start.3 = ((bf16[128,64,128]{2,0,1:T(8,128)(2,1)}), bf16[128,64,128]{2,0,1:T(8,128)(2,1)S(1)}, u32[]{:S(2)}, u32[]{:S(2)}) async-start(bf16[128,64,128]{2,0,1:T(8,128)(2,1)} %select_bitcast_fusion), calls=%async_computation.3 | async-start | bytes 4194304 | tf_op jit(solution)/shard_map/all_to_all | solution.py:108
  120.3 51.1 %while.11 = (s32[]{:T(128)}, f32[4,2048,128]{1,2,0:T(8,128)}, bf16[4,8,128,128]{2,3,1,0:T(8,128)(2,1)}, bf16[4,2048,128]{1,2,0:T(8,128)(2,1)}, bf16[4,8,128,128]...) while((s32[]{:T(128)}, f32[4,2048,128]{1,2,0:T(8,128)}, bf16[4,8,128,128]{2,3,1,0:T(8,128)(2,1)}, ...), condition=%wide.region_10.13_spmd.clone, body=%wide.region_7.12_spmd.clone.sunk | while | flops 1086588928 | bytes 19409484 | solution.py:88
  120.6 7.3 %fusion.71 = (f32[8,128]{1,0:T(8,128)S(1)}, f32[8,128,2048]{2,1,0:T(8,128)}) fusion(pred[128,2048]{1,0:T(8,128)(4,1)S(1)} %iota_compare_fusion.5, bf16[4,2048,128]{1,2,0:T(8,128)(2,1)} %get-tuple-element.189, s32[]{:T(128)} %get-tuple-element.179, bf16[4,8,128,128]{2,3,1,0:T(8,128)(2,1)} %get-tuple-element.188), kind=kOutput, calls=%fused_computation.76.clone.1 | convolution fusion | flops 545261568 | bytes 9442304 | tf_op jit(solution)/shard_map/while/body/eval_jaxpr/sub | solution.py:84
  127.8 5.4 %fusion.72 = f32[4,2048,128]{1,2,0:T(8,128)} fusion(f32[4,2048,128]{1,2,0:T(8,128)} %get-tuple-element.180, s32[]{:T(128)} %get-tuple-element.179, f32[8,128,2048]{2,1,0:T(8,128)} %get-tuple-element.170, f32[8,128]{1,0:T(8,128)S(1)} %get-tuple-element.171, bf16[4,8,128,128]{2,3,1,0:T(8,128)(2,1)} %get-tuple-element.190), kind=kOutput, calls=%fused_computation.18.clone.1 | convolution fusion | flops 541065216 | bytes 9704448 | tf_op jit(solution)/shard_map/while/body/eval_jaxpr/htu,htd->ud/dot_general | solution.py:86
  133.4 7.3 %fusion.71 = (f32[8,128]{1,0:T(8,128)S(1)}, f32[8,128,2048]{2,1,0:T(8,128)}) fusion(pred[128,2048]{1,0:T(8,128)(4,1)S(1)} %iota_compare_fusion.5, bf16[4,2048,128]{1,2,0:T(8,128)(2,1)} %get-tuple-element.189, s32[]{:T(128)} %get-tuple-element.179, bf16[4,8,128,128]{2,3,1,0:T(8,128)(2,1)} %get-tuple-element.188), kind=kOutput, calls=%fused_computation.76.clone.1 | convolution fusion | flops 545261568 | bytes 9442304 | tf_op jit(solution)/shard_map/while/body/eval_jaxpr/sub | solution.py:84
  140.7 5.3 %fusion.72 = f32[4,2048,128]{1,2,0:T(8,128)} fusion(f32[4,2048,128]{1,2,0:T(8,128)} %get-tuple-element.180, s32[]{:T(128)} %get-tuple-element.179, f32[8,128,2048]{2,1,0:T(8,128)} %get-tuple-element.170, f32[8,128]{1,0:T(8,128)S(1)} %get-tuple-element.171, bf16[4,8,128,128]{2,3,1,0:T(8,128)(2,1)} %get-tuple-element.190), kind=kOutput, calls=%fused_computation.18.clone.1 | convolution fusion | flops 541065216 | bytes 9704448 | tf_op jit(solution)/shard_map/while/body/eval_jaxpr/htu,htd->ud/dot_general | solution.py:86
  146.2 7.3 %fusion.71 = (f32[8,128]{1,0:T(8,128)S(1)}, f32[8,128,2048]{2,1,0:T(8,128)}) fusion(pred[128,2048]{1,0:T(8,128)(4,1)S(1)} %iota_compare_fusion.5, bf16[4,2048,128]{1,2,0:T(8,128)(2,1)} %get-tuple-element.189, s32[]{:T(128)} %get-tuple-element.179, bf16[4,8,128,128]{2,3,1,0:T(8,128)(2,1)} %get-tuple-element.188), kind=kOutput, calls=%fused_computation.76.clone.1 | convolution fusion | flops 545261568 | bytes 9442304 | tf_op jit(solution)/shard_map/while/body/eval_jaxpr/sub | solution.py:84
  153.4 5.3 %fusion.72 = f32[4,2048,128]{1,2,0:T(8,128)} fusion(f32[4,2048,128]{1,2,0:T(8,128)} %get-tuple-element.180, s32[]{:T(128)} %get-tuple-element.179, f32[8,128,2048]{2,1,0:T(8,128)} %get-tuple-element.170, f32[8,128]{1,0:T(8,128)S(1)} %get-tuple-element.171, bf16[4,8,128,128]{2,3,1,0:T(8,128)(2,1)} %get-tuple-element.190), kind=kOutput, calls=%fused_computation.18.clone.1 | convolution fusion | flops 541065216 | bytes 9704448 | tf_op jit(solution)/shard_map/while/body/eval_jaxpr/htu,htd->ud/dot_general | solution.py:86
  158.9 7.3 %fusion.71 = (f32[8,128]{1,0:T(8,128)S(1)}, f32[8,128,2048]{2,1,0:T(8,128)}) fusion(pred[128,2048]{1,0:T(8,128)(4,1)S(1)} %iota_compare_fusion.5, bf16[4,2048,128]{1,2,0:T(8,128)(2,1)} %get-tuple-element.189, s32[]{:T(128)} %get-tuple-element.179, bf16[4,8,128,128]{2,3,1,0:T(8,128)(2,1)} %get-tuple-element.188), kind=kOutput, calls=%fused_computation.76.clone.1 | convolution fusion | flops 545261568 | bytes 9442304 | tf_op jit(solution)/shard_map/while/body/eval_jaxpr/sub | solution.py:84
  166.2 5.3 %fusion.72 = f32[4,2048,128]{1,2,0:T(8,128)} fusion(f32[4,2048,128]{1,2,0:T(8,128)} %get-tuple-element.180, s32[]{:T(128)} %get-tuple-element.179, f32[8,128,2048]{2,1,0:T(8,128)} %get-tuple-element.170, f32[8,128]{1,0:T(8,128)S(1)} %get-tuple-element.171, bf16[4,8,128,128]{2,3,1,0:T(8,128)(2,1)} %get-tuple-element.190), kind=kOutput, calls=%fused_computation.18.clone.1 | convolution fusion | flops 541065216 | bytes 9704448 | tf_op jit(solution)/shard_map/while/body/eval_jaxpr/htu,htd->ud/dot_general | solution.py:86
  171.5 7.6 %all-to-all-start.5 = ((f32[4,64,512]{2,0,1:T(4,128)}), f32[4,64,512]{2,0,1:T(4,128)}, u32[]{:S(2)}, u32[]{:S(2)}) async-start(f32[4,64,512]{2,0,1:T(4,128)} %get-tuple-element.129), calls=%async_computation.5 | async-start | bytes 1048576 | tf_op jit(solution)/shard_map/all_to_all | solution.py:125
  179.0 111.6 %all-reduce.1 = bf16[4,2048,128]{1,2,0:T(8,128)(2,1)} all-reduce(f32[4,2048,128]{1,2,0:T(8,128)} %get-tuple-element.38), channel_id=1, replica_groups=mesh['rep'=32,'shard'=16] {'shard'}, use_global_device_ids=true, to_apply=%region_11.14 | all-reduce | flops 1048576 | bytes 6291456 | tf_op jit(solution)/shard_map/psum | solution.py:102
  295.7 13.5 %all-to-all-start.4 = ((f32[32,4,4,512]{3,2,1,0:T(4,128)}), f32[32,4,4,512]{3,2,1,0:T(4,128)S(1)}, u32[]{:S(2)}, u32[]{:S(2)}) async-start(f32[32,4,4,512]{3,2,1,0:T(4,128)} %reshape_reshape.7), calls=%async_computation.4 | async-start | bytes 2097152 | tf_op jit(solution)/shard_map/all_to_all | solution.py:40
  310.5 31.6 %all-to-all-done.4 = f32[32,4,4,512]{3,2,1,0:T(4,128)S(1)} async-done(((f32[32,4,4,512]{3,2,1,0:T(4,128)}), f32[32,4,4,512]{3,2,1,0:T(4,128)S(1)}, u32[]{:S(2)}, u32[]{:S(2)}) %all-to-all-start.4) | async-done | bytes 1048608 | tf_op jit(solution)/shard_map/all_to_all | solution.py:40
  343.1 4.8 %all-to-all-start.6 = ((bf16[16,4,4,512]{3,1,2,0:T(4,128)(2,1)}), bf16[16,4,4,512]{3,1,2,0:T(4,128)(2,1)S(1)}, u32[]{:S(2)}, u32[]{:S(2)}) async-start(bf16[16,4,4,512]{3,1,2,0:T(4,128)(2,1)} %broadcast_in_dim.144), calls=%async_computation.6 | async-start | bytes 524288 | tf_op jit(solution)/shard_map/all_to_all | solution.py:25
  349.8 8.1 %all-to-all-done.6 = bf16[16,4,4,512]{3,1,2,0:T(4,128)(2,1)S(1)} async-done(((bf16[16,4,4,512]{3,1,2,0:T(4,128)(2,1)}), bf16[16,4,4,512]{3,1,2,0:T(4,128)(2,1)S(1)}, u32[]{:S(2)}, u32[]{:S(2)}) %all-to-all-start.6) | async-done | bytes 262176 | tf_op jit(solution)/shard_map/all_to_all | solution.py:25
  (70 shorter events, 30.5 us)
Async XLA Ops:
  0.6 6.5 %copy-start = (f32[4,6,512]{2,0,1:T(4,128)S(1)}, f32[4,6,512]{2,0,1:T(4,128)}, u32[]{:S(2)}) copy-start(f32[4,6,512]{2,0,1:T(4,128)} %param.22) | copy-start | bytes 147460
  0.6 7.3 %copy-start.2 = (f32[4,6,512]{2,0,1:T(4,128)S(1)}, f32[4,6,512]{2,0,1:T(4,128)}, u32[]{:S(2)}) copy-start(f32[4,6,512]{2,0,1:T(4,128)} %param.23) | copy-start | bytes 147460
  0.7 8.2 %copy-start.3 = (f32[4,6,512]{2,0,1:T(4,128)S(1)}, f32[4,6,512]{2,0,1:T(4,128)}, u32[]{:S(2)}) copy-start(f32[4,6,512]{2,0,1:T(4,128)} %param.21) | copy-start | bytes 147460
  9.7 11.5 %copy-start.6 = (bf16[128,512]{1,0:T(8,128)(2,1)S(1)}, bf16[128,512]{1,0:T(8,128)(2,1)}, u32[]{:S(2)}) copy-start(bf16[128,512]{1,0:T(8,128)(2,1)} %param.16) | copy-start | bytes 393220
  11.4 25.3 %all-to-all-start = ((f32[4,64,512]{2,0,1:T(4,128)}), f32[4,64,512]{2,0,1:T(4,128)S(1)}, u32[]{:S(2)}, u32[]{:S(2)}) async-start(f32[4,64,512]{2,0,1:T(4,128)} %get-tuple-element.130), calls=%async_computation | async-start | bytes 1048576 | tf_op jit(solution)/shard_map/all_to_all | solution.py:123
  89.8 23.0 %all-to-all-start.1 = ((f32[4,64,512]{2,0,1:T(4,128)}), f32[4,64,512]{2,0,1:T(4,128)S(1)}, u32[]{:S(2)}, u32[]{:S(2)}) async-start(f32[4,64,512]{2,0,1:T(4,128)} %get-tuple-element.128), calls=%async_computation.1 | async-start | bytes 1048576 | tf_op jit(solution)/shard_map/all_to_all | solution.py:124
  100.5 2.4 copy-start.5
  106.8 2.3 copy-start.1
  112.8 58.6 %all-to-all-start.3 = ((bf16[128,64,128]{2,0,1:T(8,128)(2,1)}), bf16[128,64,128]{2,0,1:T(8,128)(2,1)S(1)}, u32[]{:S(2)}, u32[]{:S(2)}) async-start(bf16[128,64,128]{2,0,1:T(8,128)(2,1)} %select_bitcast_fusion), calls=%async_computation.3 | async-start | bytes 4194304 | tf_op jit(solution)/shard_map/all_to_all | solution.py:108
  171.5 124.2 %all-to-all-start.5 = ((f32[4,64,512]{2,0,1:T(4,128)}), f32[4,64,512]{2,0,1:T(4,128)}, u32[]{:S(2)}, u32[]{:S(2)}) async-start(f32[4,64,512]{2,0,1:T(4,128)} %get-tuple-element.129), calls=%async_computation.5 | async-start | bytes 1048576 | tf_op jit(solution)/shard_map/all_to_all | solution.py:125
  290.6 1.6 copy-start.4
  295.7 46.4 %all-to-all-start.4 = ((f32[32,4,4,512]{3,2,1,0:T(4,128)}), f32[32,4,4,512]{3,2,1,0:T(4,128)S(1)}, u32[]{:S(2)}, u32[]{:S(2)}) async-start(f32[32,4,4,512]{3,2,1,0:T(4,128)} %reshape_reshape.7), calls=%async_computation.4 | async-start | bytes 2097152 | tf_op jit(solution)/shard_map/all_to_all | solution.py:40
  343.1 14.8 %all-to-all-start.6 = ((bf16[16,4,4,512]{3,1,2,0:T(4,128)(2,1)}), bf16[16,4,4,512]{3,1,2,0:T(4,128)(2,1)S(1)}, u32[]{:S(2)}, u32[]{:S(2)}) async-start(bf16[16,4,4,512]{3,1,2,0:T(4,128)(2,1)} %broadcast_in_dim.144), calls=%async_computation.6 | async-start | bytes 524288 | tf_op jit(solution)/shard_map/all_to_all | solution.py:25
where the time goes:
time: 361 us; the launch traced here: 360 us
  blocking collectives  164 us (45%)
  waiting for transfers between devices  55 us (15%)
  matrix products  51.5 us (14%)
  starting transfers between devices  47.6 us (13%)
  local copies, waits for them, and re-layouts  30 us (8%)
  other arithmetic  10.2 us (3%)
    psum x1, blocking collectives, local(): values = lax.psum(value_part, 'shard').astype(jnp.bfloat16)  112 us
    all_to_all x1, blocking collectives, from_everyone(): return lax.all_to_all(copies, axis, split_axis=0, concat_axis=0, tiled=True)  52.8 us
    all_to_all x1, waiting for transfers between devices, sent_and_summed(): lax.all_to_all(parts, axis, split_axis=0, concat_axis=0, tiled=True)  31.6 us
    sub x4, matrix products, one_group(): weights = jnp.exp(scores - highest)  29.1 us
    dot_general x4, matrix products, one_group(): jnp.einsum('htu,htd->ud', probs, cotangent, preferred_element_type=jnp.fl...  21.1 us
    all_to_all x1, waiting for transfers between devices, local(): lax.all_to_all(sent_param, 'shard', split_axis=1, concat_axis=0, tiled=True)  15.3 us
    all_to_all x1, starting transfers between devices, sent_and_summed(): lax.all_to_all(parts, axis, split_axis=0, concat_axis=0, tiled=True)  13.5 us
    unnamed x22, local copies, waits for them, and re-layouts  11.8 us
  transfers between devices with their start and end apart: 6, of which 3 were waited for; matrix products, arithmetic and copies ran while one was open for 21% of the time, Pallas kernels for 0%

commit v1 on v0

--- a/solution.py
+++ b/solution.py
@@ -99,7 +99,7 @@
     columns = KV * HD
     keys_all = collect(keys, "shard", 0)
     value_part = value_terms(queries, keys_all, grad_out, shard_index * rows_here)
-    values = lax.psum(value_part, "shard").astype(jnp.bfloat16)
+    values = jnp.sum(lax.all_gather(value_part, "shard"), axis=0).astype(jnp.bfloat16)
     slot_block, slot_valid = slot_table(new_owner, shards, new_capacity)
     pieces = inputs.reshape(rows_here, blocks, block_rows)
     outgoing = jnp.where(

time: 361 us -> 1010 us (2.80)
  blocking collectives: 164 us -> 751 us
  waiting for transfers between devices: 55 us -> 84.2 us
  other arithmetic: 10.2 us -> 30.6 us
  between operations: 0.93 us -> 14.4 us
    all_to_all x1 -> x2, blocking collectives: 52.8 us -> 751 us  [the longest x1 699 us: local(): lax.all_to_all(sent_second, 'shard', split_axis=1, concat_axis=0, tiled=T...]
    psum x1 -> x0, blocking collectives: 112 us -> none  [local(): values = lax.psum(value_part, 'shard').astype(jnp.bfloat16)]
    all_to_all x1 -> x2, waiting for transfers between devices: 8.07 us -> 48 us  [from_everyone(): return lax.all_to_all(copies, axis, split_axis=0, concat_axis=0, tiled=True)]
    reduce_sum x0 -> x1, other arithmetic: none -> 22.4 us  [local(): jnp.sum(lax.all_gather(value_part, 'shard'), axis=0).astype(jnp.bfloat16)]
    all_to_all x2 -> x0, starting transfers between devices: 15.1 us -> none  [the longest x1 7.55 us: local(): lax.all_to_all(sent_second, 'shard', split_axis=1, concat_axis=0, tiled=T...]
    all_to_all x1 -> x2, starting transfers between devices: 4.77 us -> 17.4 us  [from_everyone(): return lax.all_to_all(copies, axis, split_axis=0, concat_axis=0, tiled=True)]
    all_to_all x1, waiting for transfers between devices: 15.3 us -> 4.61 us  [local(): lax.all_to_all(sent_param, 'shard', split_axis=1, concat_axis=0, tiled=True)]
  transfers between devices with their start and end apart: 6 -> 6, of which waited for: 3 -> 4; matrix products, arithmetic and copies ran while one was open for 21% -> 5% of each run, Pallas kernels for 0% -> 0%
where the time goes in v1:
time: 1010 us
  blocking collectives  751 us (74%)
  waiting for transfers between devices  84.2 us (8%)
  matrix products  54.9 us (5%)
  starting transfers between devices  40.3 us (4%)
  local copies, waits for them, and re-layouts  32.9 us (3%)
  other arithmetic  30.6 us (3%)
  between operations  14.4 us (1%)
    all_to_all x1, blocking collectives, local(): lax.all_to_all(sent_second, 'shard', split_axis=1, concat_axis=0, tiled=T...  699 us
    all_to_all x1, blocking collectives, local(): lax.all_to_all(outgoing, 'shard', split_axis=1, concat_axis=0, tiled=True)  52.1 us
    all_to_all x2, waiting for transfers between devices, from_everyone(): return lax.all_to_all(copies, axis, split_axis=0, concat_axis=0, tiled=True)  48 us
    all_to_all x1, waiting for transfers between devices, sent_and_summed(): lax.all_to_all(parts, axis, split_axis=0, concat_axis=0, tiled=True)  31.6 us
    sub x4, matrix products, one_group(): weights = jnp.exp(scores - highest)  28.4 us
    dot_general x4, matrix products, one_group(): jnp.einsum('htu,htd->ud', probs, cotangent, preferred_element_type=jnp.fl...  23.6 us
    reduce_sum x1, other arithmetic, local(): jnp.sum(lax.all_gather(value_part, 'shard'), axis=0).astype(jnp.bfloat16)  22.4 us
  transfers between devices with their start and end apart: 6, of which 4 were waited for; matrix products, arithmetic and copies ran while one was open for 5% of the time, Pallas kernels for 0%

profile of v1, /device:TPU:8, one launch (start us, length us, event | category | flops | bytes accessed | tf_op | source)
XLA Modules:
  0.0 1008.4 jit_solution(7724897488603187673)
XLA Ops:
  10.0 10.0 all-to-all-start.2
  23.0 39.9 %all-to-all-done.2 = bf16[16,128,512]{1,2,0:T(8,128)(2,1)S(1)} async-done(((bf16[16,128,512]{1,2,0:T(8,128)(2,1)}), bf16[16,128,512]{1,2,0:T(8,128)(2,1)S(1)}, u32[]{:S(2)}, u32[]{:S(2)}) %all-to-all-start.2) | async-done | bytes 2097184 | tf_op jit(solution)/shard_map/all_to_all | solution.py:25
  65.7 2.8 reshape_reshape.6
  68.5 52.9 %while.11 = (s32[]{:T(128)}, f32[4,2048,128]{2,1,0:T(8,128)}, bf16[4,8,128,128]{2,3,1,0:T(8,128)(2,1)}, bf16[4,2048,128]{1,2,0:T(8,128)(2,1)S(1)}, bf16[4,8,128,...) while((s32[]{:T(128)}, f32[4,2048,128]{2,1,0:T(8,128)}, ...), condition=%wide.region_10.13_spmd.clone, body=%wide.region_7.12_spmd.clone.sunk | while | flops 1086588928 | bytes 19409484 | solution.py:88
  68.7 7.1 fusion.71
  75.8 5.9 fusion.72
  81.9 7.1 fusion.71
  89.0 5.9 fusion.72
  95.2 7.1 fusion.71
  102.3 5.9 fusion.72
  108.4 7.1 fusion.71
  115.5 5.9 fusion.72
  130.6 699.0 %all_to_all.69 = f32[4,64,512]{2,0,1:T(4,128)} all-to-all(f32[4,64,512]{2,0,1:T(4,128)S(1)} %get-tuple-element.129), channel_id=1, replica_groups=mesh['rep'=32,'shard'=16] {'shard'}, dimensions={1} | all-to-all | bytes 1048576 | tf_op jit(solution)/shard_map/all_to_all | solution.py:125
  829.6 3.9 all-to-all-start
  836.0 3.2 copy.84
  843.4 4.6 all-to-all-done
  848.0 52.1 %all_to_all.70 = bf16[128,64,128]{2,0,1:T(8,128)(2,1)} all-to-all(bf16[128,64,128]{2,0,1:T(8,128)(2,1)S(1)} %select_bitcast_fusion), channel_id=1, replica_groups=mesh['rep'=32,'shard'=16] {'shard'}, dimensions={1} | all-to-all | bytes 4194304 | tf_op jit(solution)/shard_map/all_to_all | solution.py:108
  900.2 4.7 all-to-all-start.1
  906.6 22.4 %reduce_sum.100 = bf16[4,2048,128]{2,1,0:T(8,128)(2,1)} reduce(f32[16,4,2048,128]{3,2,1,0:T(8,128)} %bitcast.9, f32[]{:T(128)} %constant.71.clone.1), dimensions={0}, to_apply=%region_11.14 | reduce | flops 15728640 | bytes 69206016 | tf_op jit(solution)/shard_map/reduce_sum | solution.py:102
  929.1 2.9 fusion.43
  934.2 14.2 %all-to-all-start.4 = ((f32[32,4,4,512]{3,2,1,0:T(4,128)}), f32[32,4,4,512]{3,2,1,0:T(4,128)S(1)}, u32[]{:S(2)}, u32[]{:S(2)}) async-start(f32[32,4,4,512]{3,2,1,0:T(4,128)} %reshape_reshape.7), calls=%async_computation.4 | async-start | bytes 2097152 | tf_op jit(solution)/shard_map/all_to_all | solution.py:40
  949.7 31.6 %all-to-all-done.4 = f32[32,4,4,512]{3,2,1,0:T(4,128)S(1)} async-done(((f32[32,4,4,512]{3,2,1,0:T(4,128)}), f32[32,4,4,512]{3,2,1,0:T(4,128)S(1)}, u32[]{:S(2)}, u32[]{:S(2)}) %all-to-all-start.4) | async-done | bytes 1048608 | tf_op jit(solution)/shard_map/all_to_all | solution.py:40
  982.4 7.5 all-to-all-start.6
  991.7 8.1 all-to-all-done.6
  (78 shorter events, 35.2 us)
Async XLA Ops:
  7.2 117.4 %copy-start = (f32[4,6,512]{2,0,1:T(4,128)S(1)}, f32[4,6,512]{2,0,1:T(4,128)}, u32[]{:S(2)}) copy-start(f32[4,6,512]{2,0,1:T(4,128)} %param.22) | copy-start | bytes 147460
  10.0 10.0 copy-start.8
  10.0 53.0 %all-to-all-start.2 = ((bf16[16,128,512]{1,2,0:T(8,128)(2,1)}), bf16[16,128,512]{1,2,0:T(8,128)(2,1)S(1)}, u32[]{:S(2)}, u32[]{:S(2)}) async-start(bf16[16,128,512]{1,2,0:T(8,128)(2,1)} %broadcast_in_dim.138), calls=%async_computation.2 | async-start | bytes 4194304 | tf_op jit(solution)/shard_map/all_to_all | solution.py:25
  20.0 886.7 %all-gather.3.cloned.1.call-start = ((), (), s32[]{:S(2)}) async-start(), calls=%async_computation.7 | async-start | bytes 71303168 | tf_op jit(solution)/shard_map/all_gather | solution.py:102
  121.4 0.7 copy-start.9
  121.4 1.2 copy-start.1
  122.1 3.4 copy-start.2
  122.1 4.2 copy-start.3
  127.9 705.6 %copy-start.7 = (bf16[128,8192]{1,0:T(8,128)(2,1)S(1)}, bf16[128,8192]{1,0:T(8,128)(2,1)}, u32[]{:S(2)}) copy-start(bf16[128,8192]{1,0:T(8,128)(2,1)} %param.18) | copy-start | bytes 6291460
  829.6 18.5 %all-to-all-start = ((f32[4,64,512]{2,0,1:T(4,128)}), f32[4,64,512]{2,0,1:T(4,128)S(1)}, u32[]{:S(2)}, u32[]{:S(2)}) async-start(f32[4,64,512]{2,0,1:T(4,128)} %get-tuple-element.130), calls=%async_computation | async-start | bytes 1048576 | tf_op jit(solution)/shard_map/all_to_all | solution.py:123
  848.0 52.1 %copy-start.5 = (f32[4,64,512]{2,0,1:T(4,128)}, f32[4,64,512]{2,0,1:T(4,128)S(1)}, u32[]{:S(2)}) copy-start(f32[4,64,512]{2,0,1:T(4,128)S(1)} %all-to-all-done) | copy-start | bytes 1572868
  900.2 34.0 %all-to-all-start.1 = ((f32[4,64,512]{2,0,1:T(4,128)}), f32[4,64,512]{2,0,1:T(4,128)}, u32[]{:S(2)}, u32[]{:S(2)}) async-start(f32[4,64,512]{2,0,1:T(4,128)} %get-tuple-element.128), calls=%async_computation.1 | async-start | bytes 1048576 | tf_op jit(solution)/shard_map/all_to_all | solution.py:124
  932.6 15.9 %copy-start.4 = (f32[4,64,512]{2,0,1:T(4,128)S(1)}, f32[4,64,512]{2,0,1:T(4,128)}, u32[]{:S(2)}) copy-start(f32[4,64,512]{2,0,1:T(4,128)} %all_to_all.69) | copy-start | bytes 1572868
  932.6 15.9 %copy-start.6 = (f32[4,64,512]{2,0,1:T(4,128)S(1)}, f32[4,64,512]{2,0,1:T(4,128)}, u32[]{:S(2)}) copy-start(f32[4,64,512]{2,0,1:T(4,128)} %copy-done.5) | copy-start | bytes 1572868
  934.2 47.2 %all-to-all-start.4 = ((f32[32,4,4,512]{3,2,1,0:T(4,128)}), f32[32,4,4,512]{3,2,1,0:T(4,128)S(1)}, u32[]{:S(2)}, u32[]{:S(2)}) async-start(f32[32,4,4,512]{3,2,1,0:T(4,128)} %reshape_reshape.7), calls=%async_computation.4 | async-start | bytes 2097152 | tf_op jit(solution)/shard_map/all_to_all | solution.py:40
  982.4 17.4 %all-to-all-start.6 = ((bf16[16,4,4,512]{3,1,2,0:T(4,128)(2,1)}), bf16[16,4,4,512]{3,1,2,0:T(4,128)(2,1)S(1)}, u32[]{:S(2)}, u32[]{:S(2)}) async-start(bf16[16,4,4,512]{3,1,2,0:T(4,128)(2,1)} %broadcast_in_dim.144), calls=%async_computation.6 | async-start | bytes 524288 | tf_op jit(solution)/shard_map/all_to_all | solution.py:25
Sparse Core Ops, SparseCore 0:
  121.6 708.0 all-gather.2
